TPU v7x, 32 devices: a whole 2x2x4 slice. The times are simulated.
32 devices in a mesh: groups: 2 (over y), wide: 4 (over z), short: 2 (over x), sub: 2 (over core).
Axes of the slice: x: 2, y: 2, z: 4, core: 2. Of those that a mesh axis runs over, the one named last changes fastest.
Arguments:
- residual: bfloat16 [8, 12288], P('groups', 'wide'), parts along dimension 0, may hold values from -21 to 21
- attn_gain: bfloat16 [12288], P('wide'), may hold values from 0.099609375 to 1.8984375
- query_weight: bfloat16 [12288, 6144], P('wide', ('short', 'sub')), may hold values from -3 to 3
- key_value_weight: bfloat16 [12288, 1024], P('wide', ('short', 'sub')), may hold values from -3 to 3
- output_weight: bfloat16 [6144, 12288], P('short', ('wide', 'sub')), may hold values from -0.078125 to 0.078125
- cache_keys: bfloat16 [8, 4, 2048, 128], P('groups', 'short', ('wide', 'sub')), parts along dimension 0, may hold values from -16 to 16
- cached_value_rows: bfloat16 [8, 4, 2048, 128], P('groups', 'short', ('wide', 'sub')), parts along dimension 0, may hold values from -6 to 6
- lengths: int32 [8], P('groups'), parts along dimension 0, may hold values from 1024 to 2048, as said below
- positions: int32 [8], P('groups'), parts along dimension 0, may hold values from 2048 to 4095
- ffn_gain: bfloat16 [12288], P(('wide', 'sub')), may hold values from 0.099609375 to 1.8984375
- gate_weight: bfloat16 [12288, 14336], P(('wide', 'sub'), 'short'), may hold values from -0.0546875 to 0.0546875
- up_weight: bfloat16 [12288, 14336], P(('wide', 'sub'), 'short'), may hold values from -0.0546875 to 0.0546875
- down_weight: bfloat16 [14336, 12288], P('short', ('wide', 'sub')), may hold values from -0.046875 to 0.046875
Outputs:
- layer_out: bfloat16 [8, 12288], P('groups', ('wide', 'sub')), parts along dimension 0
There are 2 independent parts, one for each index of `groups`. A program takes and returns all parts, laid end to end along the dimension named above; an argument that names none is the same for every part. Nothing has to cross between parts.
Inputs may be any that keep to these rules, and one draw needn't show every extreme that they name: `lengths`: in every draw some answer has all 2048 rows cached.
All inputs are finite; a program needn't handle non-finite values.
Results may differ from a plain program's by a relative error of at most 0.008.
Values may be sent and summed in bfloat16 or wider, within the bound.
A program may use at most 128 MiB of HBM per device.

v0:
```python
import math

import jax
import jax.numpy as jnp
from jax import lax
from jax.sharding import PartitionSpec as P

MODEL_WIDTH = 12288


rope_base = 1000000.0
epsilon = 1e-05
neg_large = -1e30


def combined_all(part, axis, combine):
    gathered = jax.tree.map(lambda a: lax.all_gather(a, axis), part)

    def take(source):
        return jax.tree.map(lambda a: lax.dynamic_index_in_dim(a, source, 0, False), gathered)

    return lax.fori_loop(
        1, lax.axis_size(axis), lambda source, state: combine(state, take(source)), take(0)
    )


def rotate(values, positions):
    half = values.shape[-1] // 2
    freq = rope_base ** (-(jnp.arange(half, dtype=jnp.float32) * 2.0) / values.shape[-1])
    angle = positions.astype(jnp.float32)[:, None] * freq[None, :]
    cosine = jnp.cos(angle)[:, None, :]
    sine = jnp.sin(angle)[:, None, :]
    first_part = values[..., :half]
    second_part = values[..., half:]
    return jnp.concatenate(
        [first_part * cosine - second_part * sine, second_part * cosine + first_part * sine],
        axis=-1,
    )


def across_short(term):
    return lax.psum(term, "short")


def combine(first_part, second_part):
    highest = jnp.maximum(first_part[0], second_part[0])
    left_scale = jnp.exp(first_part[0] - highest)
    right_scale = jnp.exp(second_part[0] - highest)
    totals = first_part[1] * left_scale + second_part[1] * right_scale
    mixed = first_part[2] * left_scale[..., None] + second_part[2] * right_scale[..., None]
    return (highest, totals, mixed)


def per_device(
    residual,
    attn_gain,
    query_weight,
    key_value_weight,
    output_weight,
    cache_keys,
    cached_value_rows,
    lengths,
    positions,
    ffn_gain,
    gate_weight,
    up_weight,
    down_weight,
):
    answers = residual.shape[0]
    head_size = cache_keys.shape[3]
    kv_local = cache_keys.shape[1]
    rows_local = cache_keys.shape[2]
    resid = residual.astype(jnp.float32)
    normed = (resid * attn_gain.astype(jnp.float32)).astype(jnp.bfloat16)
    query_part = jnp.dot(normed, query_weight, preferred_element_type=jnp.float32)
    keyval_part = jnp.dot(normed, key_value_weight, preferred_element_type=jnp.float32)
    summed_query, summed_keyval, squares = lax.psum(
        (query_part, keyval_part, jnp.sum(resid * resid, axis=1)), "wide"
    )
    factor = lax.rsqrt(squares / MODEL_WIDTH + epsilon)[:, None]
    query_rows = rotate((factor * summed_query).reshape(answers, -1, head_size), positions).astype(
        jnp.bfloat16
    )
    blocks = (factor * summed_keyval).reshape(answers, -1, head_size)
    count = blocks.shape[1]
    first_block = (lax.axis_index("short") * lax.axis_size("sub") + lax.axis_index("sub")) * count
    is_key = ((first_block + jnp.arange(count, dtype=jnp.int32)) % 2 == 0)[None, :, None]
    blocks = jnp.where(is_key, rotate(blocks, positions), blocks).astype(jnp.bfloat16)
    query_rows, blocks = (
        lax.all_gather(query_rows, "sub", axis=1, tiled=True),
        lax.all_gather(blocks, "sub", axis=1, tiled=True),
    )
    key_value_rows = blocks.reshape(answers, kv_local, 2, head_size)
    new_keys = key_value_rows[:, :, 0]
    new_values = key_value_rows[:, :, 1]
    group_index = query_rows.shape[1] // kv_local
    grouped_rows = query_rows.reshape(answers, kv_local, group_index, head_size)
    scaling = 1.0 / math.sqrt(head_size)
    scores = (
        jnp.einsum("bhgd,bhrd->bhgr", grouped_rows, cache_keys, preferred_element_type=jnp.float32)
        * scaling
    )
    first_row = (lax.axis_index("wide") * lax.axis_size("sub") + lax.axis_index("sub")) * rows_local
    valid = ((first_row + jnp.arange(rows_local, dtype=jnp.int32))[None, :] < lengths[:, None])[
        :, None, None, :
    ]
    scores = jnp.where(valid, scores, neg_large)
    local_top = jnp.max(scores, axis=-1)
    weights = jnp.where(valid, jnp.exp(scores - local_top[..., None]), 0.0).astype(jnp.bfloat16)
    totals = jnp.sum(weights.astype(jnp.float32), axis=-1)
    mixed = jnp.einsum(
        "bhgr,bhrd->bhgd", weights, cached_value_rows, preferred_element_type=jnp.float32
    )
    merged_top, totals, mixed = combined_all((local_top, totals, mixed), ("wide", "sub"), combine)
    own = (
        jnp.sum(
            grouped_rows.astype(jnp.float32) * new_keys.astype(jnp.float32)[:, :, None, :], axis=-1
        )
        * scaling
    )
    highest = jnp.maximum(merged_top, own)
    rescale = jnp.exp(merged_top - highest)
    own_weight = jnp.exp(own - highest)
    numerator = (
        mixed * rescale[..., None]
        + own_weight[..., None] * new_values.astype(jnp.float32)[:, :, None, :]
    )
    attended = (
        (numerator / (totals * rescale + own_weight)[..., None])
        .reshape(answers, -1)
        .astype(jnp.bfloat16)
    )
    out_columns = output_weight.shape[1]
    resid_part = lax.dynamic_slice_in_dim(
        resid, lax.axis_index("sub") * out_columns, out_columns, 1
    )
    hidden = resid_part + across_short(
        jnp.dot(attended, output_weight, preferred_element_type=jnp.float32)
    )
    normed2 = (hidden * ffn_gain.astype(jnp.float32)).astype(jnp.bfloat16)
    gate_part = jnp.dot(normed2, gate_weight, preferred_element_type=jnp.float32)
    up_part = jnp.dot(normed2, up_weight, preferred_element_type=jnp.float32)
    squares2 = jnp.sum(hidden * hidden, axis=1)
    gate, upward, squares2 = lax.psum((gate_part, up_part, squares2), ("wide", "sub"))
    factor2 = lax.rsqrt(squares2 / MODEL_WIDTH + epsilon)[:, None]
    activated = (jax.nn.silu(factor2 * gate) * (factor2 * upward)).astype(jnp.bfloat16)
    projected = jnp.dot(activated, down_weight, preferred_element_type=jnp.float32)
    return (hidden + across_short(projected)).astype(jnp.bfloat16)


def solution(mesh):
    placed = (
        P("groups", "wide"),
        P("wide"),
        P("wide", ("short", "sub")),
        P("wide", ("short", "sub")),
        P("short", ("wide", "sub")),
        P("groups", "short", ("wide", "sub"), None),
        P("groups", "short", ("wide", "sub"), None),
        P("groups"),
        P("groups"),
        P(("wide", "sub")),
        P(("wide", "sub"), "short"),
        P(("wide", "sub"), "short"),
        P("short", ("wide", "sub")),
    )
    return jax.shard_map(
        per_device,
        mesh=mesh,
        in_specs=placed,
        out_specs=P("groups", ("wide", "sub")),
        check_vma=False,
    )
```

profile of v0, /device:TPU:0, one launch (start us, length us, event | category | flops | bytes accessed | tf_op | source)
XLA Modules:
  0.0 197.7 jit_solution(17290634108983908903)
XLA Ops:
  6.5 0.0 copy-start
  6.5 0.0 copy-start.2
  6.5 0.0 all-reduce.4.cloned.1.call-start
  6.6 1.0 multiply_reduce_fusion.1
  7.5 0.7 convert_element_type.49
  8.3 0.7 convert_element_type.50
  9.0 5.0 %fusion.13 = f32[4,1536]{1,0:T(4,128)S(1)} fusion(bf16[3072,1536]{1,0:T(8,128)(2,1)} %param.17, f32[3072]{0:T(1024)S(1)} %convert_element_type.50, bf16[4,3072]{1,0:T(4,128)(2,1)} %param.15), kind=kOutput, calls=%fused_computation.33 | convolution fusion | flops 37785600 | bytes 9498624 | tf_op jit(solution)/shard_map/dot_general | solution.py:75
  14.0 0.0 copy-done
  14.0 1.1 fusion.12
  15.1 20.9 %all-reduce.1 = (f32[4,1536]{1,0:T(4,128)S(1)}, f32[4]{0:T(128)S(1)}, f32[4,256]{1,0:T(4,128)S(1)}) all-reduce(f32[4,1536]{1,0:T(4,128)S(1)} %fusion.13, f32[4]{0:T(128)S(1)} %multiply_reduce_fusion.1, f32[4,256]{1,0:T(4,128)S(1)} %fusion.12), channel_id=1, replica_groups=mesh['groups'=2,'wide'=4,'short'=2,'sub'=2] {'wide'}, use_global_device_ids=true, to_apply=%region_2.0 | all-reduce | flops 7172 | bytes 57376 | tf_op jit(solution)/shard_map/psum | solution.py:77
  36.0 0.1 broadcast_multiply_fusion
  36.1 0.7 convert_element_type.52
  36.7 0.1 multiply_cosine_fusion
  36.8 0.1 subtract_convert_fusion
  36.9 0.1 pad_maximum_fusion
  37.0 1.8 all_gather.24
  38.8 0.7 broadcast_compare_fusion
  39.6 1.4 fusion.29
  40.9 14.0 %all-gather = f32[32,2,12]{2,1,0:T(2,128)S(1)} all-gather(f32[4,2,12]{2,1,0:T(2,128)S(1)} %get-tuple-element.243), channel_id=2, replica_groups=mesh['groups'=2,'wide'=4,'short'=2,'sub'=2] {'wide','sub'}, dimensions={0}, use_global_device_ids=true | all-gather | bytes 3456 | tf_op jit(solution)/shard_map/all_gather | solution.py:17
  54.9 0.2 convert_reduce_fusion
  55.1 14.0 %all-gather.1 = f32[32,2,12]{2,1,0:T(2,128)S(1)} all-gather(f32[4,2,12]{2,1,0:T(2,128)S(1)} %convert_reduce_fusion), channel_id=3, replica_groups=mesh['groups'=2,'wide'=4,'short'=2,'sub'=2] {'wide','sub'}, dimensions={0}, use_global_device_ids=true | all-gather | bytes 3456 | tf_op jit(solution)/shard_map/all_gather | solution.py:17
  69.1 1.3 fusion.14
  70.5 14.5 %all-gather.2 = f32[32,2,12,128]{3,1,2,0:T(2,128)S(1)} all-gather(f32[4,2,12,128]{3,1,2,0:T(2,128)S(1)} %copy.41), channel_id=4, replica_groups=mesh['groups'=2,'wide'=4,'short'=2,'sub'=2] {'wide','sub'}, dimensions={0}, use_global_device_ids=true | all-gather | bytes 442368 | tf_op jit(solution)/shard_map/all_gather | solution.py:17
  85.0 1.3 while.19
  85.1 0.1 fusion.43
  85.3 0.1 fusion.43
  85.5 0.1 fusion.43
  85.7 0.1 fusion.43
  85.9 0.1 fusion.43
  86.1 0.1 fusion.43
  86.3 0.1 fusion.43
  86.4 0.1 multiply_bitcast_fusion
  86.4 0.1 multiply_subtract_fusion
  86.5 0.1 fusion.17
  86.6 1.8 all_gather.31
  88.5 0.1 multiply_reduce_fusion
  88.6 0.1 copy.50
  88.6 0.1 mul.334
  88.7 0.1 divide_convert_fusion
  88.9 5.0 %fusion.30 = f32[4,1536]{1,0:T(4,128)S(1)} fusion(bf16[4,3072]{1,0:T(4,128)(2,1)S(1)} %convert_element_type.58, bf16[3072,1536]{1,0:T(8,128)(2,1)} %param.19), kind=kOutput, calls=%fused_computation.68 | convolution fusion | flops 37748736 | bytes 9486336 | tf_op jit(solution)/shard_map/dot_general | solution.py:138
  93.9 8.3 %psum.59 = f32[4,1536]{1,0:T(4,128)S(1)} all-reduce(f32[4,1536]{1,0:T(4,128)S(1)} %fusion.30), channel_id=1, replica_groups=mesh['groups'=2,'wide'=4,'short'=2,'sub'=2] {'short'}, use_global_device_ids=true, to_apply=%region_9.10 | all-reduce | flops 6144 | bytes 49152 | tf_op jit(solution)/shard_map/psum | solution.py:42
  102.2 0.0 copy-done.2
  102.2 0.1 multiply_reduce_fusion.2
  102.3 0.0 copy-start.1
  102.3 9.6 %fusion.24 = f32[4,7168]{1,0:T(4,128)} fusion(bf16[1536,7168]{1,0:T(8,128)(2,1)} %param.26, f32[4,1536]{1,0:T(4,128)S(1)} %get-tuple-element.231, f32[1536]{0:T(1024)S(1)} %convert_element_type.59), kind=kOutput, calls=%fused_computation.65 | convolution fusion | flops 88092672 | bytes 22165504 | tf_op jit(solution)/shard_map/dot_general | solution.py:142
  111.9 9.4 %fusion.25 = f32[4,7168]{1,0:T(4,128)} fusion(bf16[1536,7168]{1,0:T(8,128)(2,1)} %param.25, f32[4,1536]{1,0:T(4,128)S(1)} %get-tuple-element.231, f32[1536]{0:T(1024)S(1)} %convert_element_type.59), kind=kOutput, calls=%fused_computation.66 | convolution fusion | flops 88092672 | bytes 22165504 | tf_op jit(solution)/shard_map/dot_general | solution.py:141
  121.4 0.0 all-reduce.4.cloned.1.call-update
  121.4 13.7 %psum.60 = f32[4]{0:T(128)S(1)} all-reduce(f32[4]{0:T(128)S(1)} %get-tuple-element.230), channel_id=1, replica_groups=mesh['groups'=2,'wide'=4,'short'=2,'sub'=2] {'wide','sub'}, use_global_device_ids=true, to_apply=%region_11.12 | all-reduce | flops 4 | bytes 32 | tf_op jit(solution)/shard_map/psum | solution.py:144
  135.1 36.5 %all-reduce.4.cloned.1.call-done = (f32[4,7168]{1,0:T(4,128)}, f32[4,7168]{1,0:T(4,128)}) async-done(((f32[4,7168]{1,0:T(4,128)}, f32[4,7168]{1,0:T(4,128)}), (f32[4,7168]{1,0:T(4,128)}, f32[4,7168]{1,0:T(4,128)})) %all-reduce.4.cloned.1.call-update) | async-done | bytes 229392 | tf_op jit(solution)/shard_map/psum | solution.py:144
  171.6 10.4 %fusion.7 = f32[4,1536]{1,0:T(4,128)S(1)} fusion(bf16[7168,1536]{1,0:T(8,128)(2,1)} %param.27, f32[4,7168]{1,0:T(4,128)} %get-tuple-element.221, f32[4,7168]{1,0:T(4,128)} %get-tuple-element.222, f32[4]{0:T(128)S(1)} %add_rsqrt_fusion), kind=kOutput, calls=%fused_computation.18 | convolution fusion | flops 88309760 | bytes 22274064 | tf_op jit(solution)/shard_map/dot_general | solution.py:147
  182.0 8.3 %psum.63 = f32[4,1536]{1,0:T(4,128)S(1)} all-reduce(f32[4,1536]{1,0:T(4,128)S(1)} %fusion.7), channel_id=1, replica_groups=mesh['groups'=2,'wide'=4,'short'=2,'sub'=2] {'short'}, use_global_device_ids=true, to_apply=%region_14.15 | all-reduce | flops 6144 | bytes 49152 | tf_op jit(solution)/shard_map/psum | solution.py:42
  190.2 0.6 add_convert_fusion.1
  190.8 0.0 copy-done.1
  (33 shorter events, 0.5 us)
Async XLA Ops:
  6.5 7.5 %copy-start = (bf16[3072,256]{1,0:T(8,128)(2,1)S(1)}, bf16[3072,256]{1,0:T(8,128)(2,1)}, u32[]{:S(2)}) copy-start(bf16[3072,256]{1,0:T(8,128)(2,1)} %param.18) | copy-start | bytes 4718596
  6.5 95.7 %copy-start.2 = (bf16[1536]{0:T(1024)(128)(2,1)S(1)}, bf16[1536]{0:T(1024)(128)(2,1)}, u32[]{:S(2)}) copy-start(bf16[1536]{0:T(1024)(128)(2,1)} %param.24) | copy-start | bytes 9220
  6.5 165.0 %all-reduce.4.cloned.1.call-start = ((), (), s32[]{:S(2)}) async-start(), calls=%async_computation | async-start | bytes 458752 | tf_op jit(solution)/shard_map/psum | solution.py:144
  102.3 88.5 %copy-start.1 = (bf16[3072,256]{1,0:T(8,128)(2,1)S(1)}, bf16[3072,256]{1,0:T(8,128)(2,1)}, u32[]{:S(2)}) copy-start(bf16[3072,256]{1,0:T(8,128)(2,1)} %param.18) | copy-start | bytes 4718596
Sparse Core Ops, SparseCore 0:
  121.5 50.0 all-reduce.3
where the time goes:
time: 198 us
  blocking collectives  97.3 us (49%)
  matrix products  43.1 us (22%)
  waiting for transfers between devices  36.5 us (18%)
  between operations  13.5 us (7%)
  other arithmetic  6.62 us (3%)
    all_gather x3, blocking collectives, combined_all(): gathered = jax.tree.map(lambda a: lax.all_gather(a, axis), part)  42.6 us
    psum x1, waiting for transfers between devices, per_device(): lax.psum((gate_part, up_part, squares2), ('wide', 'sub'))  36.5 us
    psum x1, blocking collectives, per_device(): lax.psum((query_part, keyval_part, jnp.sum(resid * resid, axis=1)), 'wide')  20.9 us
    psum x2, blocking collectives, across_short(): return lax.psum(term, 'short')  16.5 us
    psum x1, blocking collectives, per_device(): lax.psum((gate_part, up_part, squares2), ('wide', 'sub'))  13.7 us
    dot_general x1, matrix products, per_device(): jnp.dot(activated, down_weight, preferred_element_type=jnp.float32)  10.4 us
    dot_general x1, matrix products, per_device(): up_part = jnp.dot(normed2, up_weight, preferred_element_type=jnp.float32)  9.57 us
    dot_general x1, matrix products, per_device(): jnp.dot(normed2, gate_weight, preferred_element_type=jnp.float32)  9.45 us
  transfers between devices with their start and end apart: 1, of which 1 were waited for; matrix products, arithmetic and copies ran while one was open for 0% of the time, Pallas kernels for 0%

commit v1 on v0

v1 whole, which is shorter than its diff:
```python
import functools
import math

import jax
import jax.numpy as jnp
from jax import lax
from jax.experimental import pallas as pl
from jax.experimental.pallas import tpu as pltpu
from jax.sharding import PartitionSpec as P

rope_base = 1000000.0
epsilon = 1e-05
neg_large = -1e30
lane = 128
bf16 = jnp.bfloat16
f32 = jnp.float32
weight_budget = 60 * 2**20
vmem_limit = 63 * 2**20


def split_two(value):
    high = value.astype(bf16).astype(f32)
    return high, value - high


def largest_divisor(count, most):
    return max(d for d in range(1, most + 1) if count % d == 0)


class Plan:
    def __init__(self, sizes, residual, query, keyval, output, cache, gate, down):
        self.wide, self.short, self.sub = sizes
        self.members = self.wide * self.sub
        self.answers, self.width = residual
        self.groups = 16 // self.answers
        self.model = self.width * self.wide
        self.query_cols = query[1]
        self.heads = self.query_cols // lane
        self.blocks = keyval[1] // lane
        self.head_tiles = -(-self.heads // self.groups)
        self.pack_cols = -(-(self.heads + self.blocks + 2) // self.groups) * lane
        self.kv_heads = cache[1]
        self.rows = cache[2]
        self.units = self.sub * self.head_tiles
        self.out_rows, self.out_cols = output
        self.gate_rows, self.ff = gate
        self.owners = largest_divisor(self.ff // lane, self.members)
        self.piece = self.ff // self.owners
        self.tiles = self.piece // lane
        self.half = -(-(self.tiles + 1) // self.groups) * lane
        self.query_chunks = largest_divisor(self.width // lane, 6)
        self.out_chunks = largest_divisor(self.out_rows // lane, 6)
        fixed = 2 * (
            query[0] * query[1] + keyval[0] * keyval[1] + output[0] * output[1]
            + 2 * math.prod(cache)
        )
        slot = 2 * self.gate_rows * 2 * self.piece
        self.slots = min(self.members, (weight_budget - fixed) // slot)
        in_query = self.width // self.piece if self.query_cols >= self.out_cols else 0
        in_out = self.out_rows // self.piece
        places = [("query", k) for k in range(in_query)] + [("out", k) for k in range(in_out)]
        places = places[: self.members]
        left = self.members - len(places)
        fits = self.piece <= self.gate_rows and self.out_cols <= 2 * self.piece
        kind = "slot" if fits and left <= self.slots else "extra"
        places += [(kind, k) for k in range(left)]
        self.places = places
        self.extra = max(left * self.piece, 16) if kind == "extra" else 16
        assert self.units <= self.members and self.sub % self.kv_heads == 0
        assert self.blocks * self.sub == 2 * self.kv_heads


def kernel(
    plan,
    res_ref, attn_ref, ffn_ref, len_ref, pos_ref,
    query_hbm, keyval_hbm, output_hbm, keys_hbm, values_hbm, gate_hbm, up_hbm, down_hbm,
    out_ref,
    query_buf, keyval_buf, output_buf, keys_buf, values_buf, ffn_buf, extra_buf,
    normed_ref, pack_ref, spread_ref, kv_ref, new_key_ref, new_value_ref,
    send1, recv1, rot, pay, recv_pay, att, out_lhs, wide_acc,
    part_send, part_recv, normed2_ref, hidden_ref, square_ref,
    ffn_pack, ffn_send, ffn_recv, act, down_lhs, last_send, last_recv,
    query_sem, keyval_sem, cache_sem, output_sem, ffn_sem, down_sem,
    s1, r1, s2, r2, s3, r3, s4, r4, s5, r5, s6, r6, s7, r7, s8, r8,
):
    n, wides, shorts, subs = plan.members, plan.wide, plan.short, plan.sub
    answers, groups = plan.answers, plan.groups
    wide, short, sub = lax.axis_index("wide"), lax.axis_index("short"), lax.axis_index("sub")
    me = wide * subs + sub
    all_own = plan.owners == n

    def member(rank):
        return {"wide": rank // subs, "sub": rank % subs}

    def owned(rank, body):
        if all_own:
            body()
        else:
            pl.when(rank < plan.owners)(body)

    def remote(src, dst, ssem, rsem, device):
        return pltpu.make_async_remote_copy(
            src_ref=src, dst_ref=dst, send_sem=ssem, recv_sem=rsem,
            device_id=device, device_id_type=pl.DeviceIdType.MESH,
        )

    barrier = pltpu.get_barrier_semaphore()
    for o in range(1, n):
        pl.semaphore_signal(
            barrier, inc=1, device_id=member(lax.rem(me + o, n)),
            device_id_type=pl.DeviceIdType.MESH,
        )
    for o in range(1, shorts):
        pl.semaphore_signal(
            barrier, inc=1, device_id={"short": lax.rem(short + o, shorts)},
            device_id_type=pl.DeviceIdType.MESH,
        )

    q_rows = plan.width // plan.query_chunks
    o_rows = plan.out_rows // plan.out_chunks

    def query_copy(c):
        at = pl.ds(c * q_rows, q_rows)
        return pltpu.make_async_copy(query_hbm.at[at], query_buf.at[at], query_sem.at[c])

    def output_copy(c):
        at = pl.ds(c * o_rows, o_rows)
        return pltpu.make_async_copy(output_hbm.at[at], output_buf.at[at], output_sem.at[c])

    keyval_copy = pltpu.make_async_copy(keyval_hbm, keyval_buf, keyval_sem.at[0])
    keys_copy = pltpu.make_async_copy(keys_hbm, keys_buf, cache_sem.at[0])
    values_copy = pltpu.make_async_copy(values_hbm, values_buf, cache_sem.at[1])

    def ffn_rank(i):
        return lax.rem(me + 1 + i, n)

    def ffn_copies(i):
        slot = lax.rem(i, plan.slots)
        at = pl.ds(pl.multiple_of(ffn_rank(i) * plan.piece, lane), plan.piece)
        return [
            pltpu.make_async_copy(
                hbm.at[:, at],
                ffn_buf.at[slot, :, pl.ds(k * plan.piece, plan.piece)],
                ffn_sem.at[slot, k],
            )
            for k, hbm in enumerate((gate_hbm, up_hbm))
        ]

    def ffn_start(i):
        def body():
            for copy in ffn_copies(i):
                copy.start()

        owned(ffn_rank(i), body)

    def down_rank(j):
        return lax.rem(me - j + n, n)

    def down_place(j):
        kind, k = plan.places[j]
        if kind == "slot":
            at = (n - plan.slots + k) % plan.slots
            return ffn_buf.at[at, pl.ds(0, plan.piece), pl.ds(0, plan.out_cols)]
        buf = {"query": query_buf, "out": output_buf, "extra": extra_buf}[kind]
        return buf.at[pl.ds(k * plan.piece, plan.piece), pl.ds(0, plan.out_cols)]

    def down_copy(j):
        at = pl.ds(pl.multiple_of(down_rank(j) * plan.piece, lane), plan.piece)
        return pltpu.make_async_copy(down_hbm.at[at], down_place(j), down_sem.at[j])

    def down_start(j):
        owned(down_rank(j), lambda: down_copy(j).start())

    keyval_copy.start()
    for c in range(plan.query_chunks):
        query_copy(c).start()
    keys_copy.start()
    values_copy.start()
    queue = [functools.partial(lambda c: output_copy(c).start(), c) for c in range(plan.out_chunks)]
    queue += [functools.partial(ffn_start, i) for i in range(plan.slots)]

    resid = res_ref[...].astype(f32)
    normed_ref[...] = (resid * attn_ref[...].astype(f32)).astype(bf16)
    squares = jnp.sum(resid * resid, axis=1, keepdims=True)

    row16 = lax.broadcasted_iota(jnp.int32, (16, lane), 0)
    lane16 = lax.broadcasted_iota(jnp.int32, (16, lane), 1)
    group16 = row16 // answers
    answer16 = row16 % answers
    position = jnp.zeros((16, lane), f32)
    for a in range(answers):
        position = jnp.where(answer16 == a, pos_ref[a].astype(f32), position)
    freq = jnp.exp((lane16 % (lane // 2)).astype(f32) * (-2.0 / lane * math.log(rope_base)))
    angle = position * freq
    cosine = jnp.cos(angle)
    sine = jnp.sin(angle)
    sine = jnp.where(lane16 < lane // 2, -sine, sine)
    ffn_pack[...] = jnp.zeros_like(ffn_pack)

    keyval_copy.wait()
    kv_part = jnp.dot(normed_ref[...], keyval_buf[...], preferred_element_type=f32)
    q_part = jnp.zeros((answers, plan.query_cols), f32)
    share = -(-len(queue) // plan.query_chunks)
    for c in range(plan.query_chunks):
        query_copy(c).wait()
        for _ in range(share):
            if queue:
                queue.pop(0)()
        at = pl.ds(c * q_rows, q_rows)
        q_part += jnp.dot(normed_ref[:, at], query_buf[at, :], preferred_element_type=f32)
    for j, (kind, _) in enumerate(plan.places):
        if kind in ("query", "extra"):
            down_start(j)

    def place(k):
        g, first = k % groups, k // groups * lane
        return slice(g * answers, (g + 1) * answers), slice(first, first + lane)

    def tiles_of(value):
        return [value[:, k * lane : (k + 1) * lane] for k in range(value.shape[1] // lane)]

    packed = tiles_of(q_part) + tiles_of(kv_part)
    packed += split_two(jnp.broadcast_to(squares, (answers, lane)))
    pack_ref[...] = jnp.zeros_like(pack_ref)
    for k, tile in enumerate(packed):
        pack_ref[place(k)] = tile
    send1[...] = pack_ref[...].astype(bf16)

    pl.semaphore_wait(barrier, n - 1 + shorts - 1)

    def copy1(o):
        return remote(
            send1, recv1.at[o - 1], s1.at[o - 1], r1.at[o - 1],
            {"wide": lax.rem(wide + o, wides)},
        )

    for o in range(1, wides):
        copy1(o).start()
    for o in range(1, wides):
        copy1(o).wait_recv()
        pack_ref[...] += recv1[o - 1].astype(f32)

    def spread(four):
        for g in range(groups):
            spread_ref[g * answers : (g + 1) * answers, :] = four
        return spread_ref[...]

    square_at = plan.heads + plan.blocks
    total = pack_ref[place(square_at)] + pack_ref[place(square_at + 1)]
    factor = spread(lax.rsqrt(total / plan.model + epsilon))
    for t in range(plan.pack_cols // lane):
        value = pack_ref[:, t * lane : (t + 1) * lane] * factor
        turned = value * cosine + pltpu.roll(value, lane // 2, 1) * sine
        if (t + 1) * groups > plan.heads:
            block = t * groups + group16 - plan.heads
            is_value = (block >= 0) & ((sub * plan.blocks + block + 2) % 2 == 1)
            turned = jnp.where(is_value, value, turned)
        rot[sub, :, t * lane : (t + 1) * lane] = turned.astype(bf16)

    def copy2(o, source):
        return remote(
            rot.at[source], rot.at[source], s2.at[o - 1], r2.at[o - 1],
            {"sub": lax.rem(sub + o, subs)},
        )

    for o in range(1, subs):
        copy2(o, sub).start()
    for o in range(1, subs):
        copy2(o, lax.rem(sub - o + subs, subs)).wait_recv()

    keys_copy.wait()
    values_copy.wait()
    scaling = 1.0 / math.sqrt(lane)
    heads = plan.head_tiles
    sharers = subs // plan.kv_heads
    stacked = sharers * heads * 16
    row_id = lax.broadcasted_iota(jnp.int32, (stacked, plan.rows), 0)
    col_id = lax.broadcasted_iota(jnp.int32, (stacked, plan.rows), 1) + me * plan.rows
    valid = [(row_id % answers == a) & (col_id < len_ref[a]) for a in range(answers)]

    def copy3(u, source):
        return remote(pay.at[u], recv_pay.at[source], s3.at[u], r3.at[source], member(u))

    for h in range(plan.kv_heads):
        queries = jnp.concatenate(
            [
                rot[s, :, t * lane : (t + 1) * lane]
                for s in range(h * sharers, (h + 1) * sharers)
                for t in range(heads)
            ],
            axis=0,
        )
        for k, new_ref in enumerate((new_key_ref, new_value_ref)):
            block = 2 * h + k
            rows, columns = place(plan.heads + block % plan.blocks)
            kv_ref[...] = rot[block // plan.blocks, :, columns].astype(f32)
            for g in range(groups):
                new_ref[g * answers : (g + 1) * answers, :] = kv_ref[rows, :]
        new_key = jnp.concatenate([new_key_ref[...]] * (sharers * heads), axis=0)
        new_value = jnp.concatenate([new_value_ref[...]] * (sharers * heads), axis=0)
        own = jnp.sum(queries.astype(f32) * new_key, axis=1, keepdims=True) * scaling
        scores = []
        for a in range(answers):
            score = lax.dot_general(
                queries, keys_buf[a, h], (((1,), (1,)), ((), ())), preferred_element_type=f32
            )
            scores.append(jnp.where(valid[a], score * scaling, neg_large))
        top = functools.reduce(jnp.maximum, scores)
        top = jnp.max(top, axis=1, keepdims=True)
        top = jnp.where(me == 0, jnp.maximum(top, own), top)
        own_weight = jnp.where(me == 0, jnp.exp(own - top), 0.0)
        totals = own_weight
        mixed = own_weight * new_value
        for a in range(answers):
            weights = jnp.where(valid[a], jnp.exp(scores[a] - top), 0.0).astype(bf16)
            totals += jnp.sum(weights.astype(f32), axis=1, keepdims=True)
            mixed += jnp.dot(weights, values_buf[a, h], preferred_element_type=f32)
        for t in range(sharers * heads):
            u = h * sharers * heads + t
            rows = slice(t * 16, (t + 1) * 16)
            top_high, rest = split_two(jnp.broadcast_to(top[rows], (16, lane)))
            top_mid, top_low = split_two(rest)
            sum_high, sum_low = split_two(jnp.broadcast_to(totals[rows], (16, lane)))
            stats = jnp.where(lane16 < 64, sum_high, sum_low)
            stats = jnp.where(lane16 < 48, top_low, stats)
            stats = jnp.where(lane16 < 32, top_mid, stats)
            stats = jnp.where(lane16 < 16, top_high, stats)
            pay[u, :16, :] = mixed[rows].astype(bf16)
            pay[u, 16:, :] = stats.astype(bf16)

            @pl.when(me != u)
            def _():
                copy3(u, me).start()

    def copy4(o, source):
        return remote(
            att.at[source], att.at[source], s4.at[o - 1], r4.at[source],
            member(lax.rem(me + o, n)),
        )

    @pl.when(me < plan.units)
    def _():
        parts = [pay[me].astype(f32)]
        for o in range(1, n):
            source = lax.rem(me + o, n)
            copy3(0, source).wait_recv()
            parts.append(recv_pay[source].astype(f32))
        tops = [
            p[16:, 0:1] + p[16:, 16:17] + p[16:, 32:33] for p in parts
        ]
        highest = functools.reduce(jnp.maximum, tops)
        numerator = jnp.zeros((16, lane), f32)
        denominator = jnp.zeros((16, 1), f32)
        for p, top in zip(parts, tops):
            scale = jnp.exp(top - highest)
            numerator += p[:16] * scale
            denominator += (p[16:, 48:49] + p[16:, 64:65]) * scale
        att[me] = (numerator / denominator).astype(bf16)
        for o in range(1, n):
            copy4(o, me).start()

    for u in range(plan.units):

        @pl.when(me != u)
        def _():
            copy4(1, u).wait_recv()

    for u in range(plan.units):
        block = att[u].astype(f32)
        for g in range(groups):
            head = (u % heads) * groups + g
            if head >= plan.heads:
                continue
            head += u // heads * plan.heads
            out_lhs[:, head * lane : (head + 1) * lane] = jnp.where(
                group16 == g, block, 0.0
            ).astype(bf16)
    product = jnp.zeros((16, plan.out_cols), f32)
    for c in range(plan.out_chunks):
        output_copy(c).wait()
        at = pl.ds(c * o_rows, o_rows)
        product += jnp.dot(out_lhs[:, at], output_buf[at, :], preferred_element_type=f32)
    for j, (kind, _) in enumerate(plan.places):
        if kind == "out":
            down_start(j)

    def folded(value):
        wide_acc[...] = value
        return functools.reduce(
            jnp.add, [wide_acc[g * answers : (g + 1) * answers, :] for g in range(groups)]
        )

    def across_short(value, send, recv, ssem, rsem):
        send[...] = value
        copies = [
            remote(
                send, recv.at[o - 1], ssem.at[o - 1], rsem.at[o - 1],
                {"short": lax.rem(short + o, shorts)},
            )
            for o in range(1, shorts)
        ]
        for copy in copies:
            copy.start()
        for o, copy in enumerate(copies):
            copy.wait_recv()
            value += recv[o]
        return value

    resid_part = res_ref[:, : plan.out_cols].astype(f32)
    for k in range(1, subs):
        here = res_ref[:, k * plan.out_cols : (k + 1) * plan.out_cols].astype(f32)
        resid_part = jnp.where(sub == k, here, resid_part)
    hidden = resid_part + across_short(folded(product), part_send, part_recv, s5, r5)
    hidden_ref[...] = hidden
    normed2_ref[...] = (hidden * ffn_ref[...].astype(f32)).astype(bf16)
    high, low = split_two(
        jnp.broadcast_to(jnp.sum(hidden * hidden, axis=1, keepdims=True), (answers, lane))
    )
    square_ref[0] = high
    square_ref[1] = low

    def ffn_place(t, k):
        rows, columns = place(t)
        first = columns.start + k * plan.half
        return rows, slice(first, first + lane)

    def ffn_piece(i):
        slot = lax.rem(i, plan.slots)
        for copy in ffn_copies(i):
            copy.wait()
        for k in range(2):
            part = jnp.dot(
                normed2_ref[...],
                ffn_buf[slot, :, pl.ds(k * plan.piece, plan.piece)],
                preferred_element_type=f32,
            )
            for t, tile in enumerate(tiles_of(part) + [square_ref[k]]):
                ffn_pack[ffn_place(t, k)] = tile

    def copy6(i):
        return remote(
            ffn_send.at[i], ffn_recv.at[i], s6.at[i], r6.at[i], member(ffn_rank(i))
        )

    def ffn_freed(i):
        @pl.when(i + plan.slots < n)
        def _():
            ffn_start(i + plan.slots)

        for j, (kind, k) in enumerate(plan.places):
            if kind == "slot":

                @pl.when(i == n - plan.slots + k)
                def _():
                    down_start(j)

    def ffn_step(i, carry):
        def body():
            ffn_piece(i)
            ffn_send[i] = ffn_pack[...].astype(bf16)
            copy6(i).start()

        owned(ffn_rank(i), body)
        ffn_freed(i)
        return carry

    lax.fori_loop(0, n - 1, ffn_step, 0)

    def copy7(o):
        return remote(
            act.at[n - 1], act.at[o - 1], s7.at[o - 1], r7.at[o - 1],
            member(lax.rem(me + o, n)),
        )

    def activate():
        ffn_piece(n - 1)
        for i in range(n - 1):
            copy6(i).wait_recv()
            ffn_pack[...] += ffn_recv[i].astype(f32)
        total2 = ffn_pack[ffn_place(plan.tiles, 0)] + ffn_pack[ffn_place(plan.tiles, 1)]
        factor2 = spread(lax.rsqrt(total2 / plan.model + epsilon))
        for t in range(plan.half // lane):
            gate = ffn_pack[:, t * lane : (t + 1) * lane] * factor2
            upward = ffn_pack[:, plan.half + t * lane : plan.half + (t + 1) * lane] * factor2
            act[n - 1, :, t * lane : (t + 1) * lane] = (
                gate / (1.0 + jnp.exp(-gate)) * upward
            ).astype(bf16)
        for o in range(1, n):
            copy7(o).start()

    owned(me, activate)
    ffn_freed(n - 1)

    wide_acc[...] = jnp.zeros_like(wide_acc)
    for j in range(n):

        def down_piece():
            if j:
                copy7(j).wait_recv()
            down_copy(j).wait()
            block = act[(j - 1) % n].astype(f32)
            for k in range(plan.tiles):
                first = (k // groups) * lane
                down_lhs[:, k * lane : (k + 1) * lane] = jnp.where(
                    group16 == k % groups, block[:, first : first + lane], 0.0
                ).astype(bf16)
            wide_acc[...] += jnp.dot(
                down_lhs[...], down_place(j)[...], preferred_element_type=f32
            )

        owned(down_rank(j), down_piece)
    projected = across_short(folded(wide_acc[...]), last_send, last_recv, s8, r8)
    out_ref[...] = (hidden_ref[...] + projected).astype(bf16)

    for o in range(1, wides):
        copy1(o).wait_send()
    for o in range(1, subs):
        copy2(o, sub).wait_send()
    for u in range(plan.units):

        @pl.when(me != u)
        def _():
            copy3(u, me).wait_send()

    @pl.when(me < plan.units)
    def _():
        for o in range(1, n):
            copy4(o, me).wait_send()

    for o in range(1, shorts):
        for send, recv, ssem, rsem in (
            (part_send, part_recv, s5, r5), (last_send, last_recv, s8, r8)
        ):
            remote(
                send, recv.at[o - 1], ssem.at[o - 1], rsem.at[o - 1],
                {"short": lax.rem(short + o, shorts)},
            ).wait_send()
    for i in range(n - 1):
        owned(ffn_rank(i), lambda: copy6(i).wait_send())

    def sent7():
        for o in range(1, n):
            copy7(o).wait_send()

    owned(me, sent7)


def per_device(
    sizes, residual, attn_gain, query_weight, key_value_weight, output_weight, cache_keys,
    cached_value_rows, lengths, positions, ffn_gain, gate_weight, up_weight, down_weight,
):
    plan = Plan(
        sizes, residual.shape, query_weight.shape, key_value_weight.shape, output_weight.shape,
        cache_keys.shape, gate_weight.shape, down_weight.shape,
    )
    n, answers = plan.members, plan.answers
    vmem = pl.BlockSpec(memory_space=pltpu.VMEM)
    smem = pl.BlockSpec(memory_space=pltpu.SMEM)
    hbm = pl.BlockSpec(memory_space=pltpu.HBM)
    dma = pltpu.SemaphoreType.DMA
    short_peers = max(plan.short - 1, 1)
    scratch = [
        pltpu.VMEM(query_weight.shape, bf16),
        pltpu.VMEM(key_value_weight.shape, bf16),
        pltpu.VMEM(output_weight.shape, bf16),
        pltpu.VMEM(cache_keys.shape, bf16),
        pltpu.VMEM(cache_keys.shape, bf16),
        pltpu.VMEM((plan.slots, plan.gate_rows, 2 * plan.piece), bf16),
        pltpu.VMEM((plan.extra, plan.out_cols), bf16),
        pltpu.VMEM((answers, plan.width), bf16),
        pltpu.VMEM((16, plan.pack_cols), f32),
        pltpu.VMEM((16, lane), f32),
        pltpu.VMEM((16, lane), f32),
        pltpu.VMEM((16, lane), f32),
        pltpu.VMEM((16, lane), f32),
        pltpu.VMEM((16, plan.pack_cols), bf16),
        pltpu.VMEM((plan.wide - 1, 16, plan.pack_cols), bf16),
        pltpu.VMEM((plan.sub, 16, plan.pack_cols), bf16),
        pltpu.VMEM((plan.units, 32, lane), bf16),
        pltpu.VMEM((n, 32, lane), bf16),
        pltpu.VMEM((plan.units, 16, lane), bf16),
        pltpu.VMEM((16, plan.out_rows), bf16),
        pltpu.VMEM((16, plan.out_cols), f32),
        pltpu.VMEM((answers, plan.out_cols), f32),
        pltpu.VMEM((short_peers, answers, plan.out_cols), f32),
        pltpu.VMEM((answers, plan.out_cols), bf16),
        pltpu.VMEM((answers, plan.out_cols), f32),
        pltpu.VMEM((2, answers, lane), f32),
        pltpu.VMEM((16, 2 * plan.half), f32),
        pltpu.VMEM((n - 1, 16, 2 * plan.half), bf16),
        pltpu.VMEM((n - 1, 16, 2 * plan.half), bf16),
        pltpu.VMEM((n, 16, plan.half), bf16),
        pltpu.VMEM((16, plan.piece), bf16),
        pltpu.VMEM((answers, plan.out_cols), f32),
        pltpu.VMEM((short_peers, answers, plan.out_cols), f32),
        dma((plan.query_chunks,)),
        dma((1,)),
        dma((2,)),
        dma((plan.out_chunks,)),
        dma((plan.slots, 2)),
        dma((n,)),
        dma((plan.wide - 1,)), dma((plan.wide - 1,)),
        dma((plan.sub - 1,)), dma((plan.sub - 1,)),
        dma((plan.units,)), dma((n,)),
        dma((n - 1,)), dma((plan.units,)),
        dma((short_peers,)), dma((short_peers,)),
        dma((n - 1,)), dma((n - 1,)),
        dma((n - 1,)), dma((n - 1,)),
        dma((short_peers,)), dma((short_peers,)),
    ]
    return pl.pallas_call(
        functools.partial(kernel, plan),
        out_shape=jax.ShapeDtypeStruct((answers, plan.out_cols), bf16),
        in_specs=[vmem, vmem, vmem, smem, smem] + [hbm] * 8,
        out_specs=vmem,
        scratch_shapes=scratch,
        compiler_params=pltpu.CompilerParams(
            collective_id=0, has_side_effects=True, vmem_limit_bytes=vmem_limit
        ),
        name="layer",
    )(
        residual, attn_gain.reshape(1, -1), ffn_gain.reshape(1, -1), lengths, positions,
        query_weight, key_value_weight, output_weight, cache_keys, cached_value_rows,
        gate_weight, up_weight, down_weight,
    )


def solution(mesh):
    sizes = (mesh.shape["wide"], mesh.shape["short"], mesh.shape["sub"])
    placed = (
        P("groups", "wide"),
        P("wide"),
        P("wide", ("short", "sub")),
        P("wide", ("short", "sub")),
        P("short", ("wide", "sub")),
        P("groups", "short", ("wide", "sub"), None),
        P("groups", "short", ("wide", "sub"), None),
        P("groups"),
        P("groups"),
        P(("wide", "sub")),
        P(("wide", "sub"), "short"),
        P(("wide", "sub"), "short"),
        P("short", ("wide", "sub")),
    )
    return jax.shard_map(
        functools.partial(per_device, sizes),
        mesh=mesh,
        in_specs=placed,
        out_specs=P("groups", ("wide", "sub")),
        check_vma=False,
    )
```

time: 198 us -> 52.1 us (0.26)
  blocking collectives: 97.3 us -> 0 us
  Pallas kernels: 0 us -> 47.8 us
  matrix products: 43.1 us -> 0 us
  waiting for transfers between devices: 36.5 us -> 0 us
  between operations: 13.5 us -> 0.01 us
  other arithmetic: 6.62 us -> 0 us
  local copies, waits for them, and re-layouts: 0.38 us -> 3.89 us
    psum x4 -> x0, blocking collectives: 51.1 us -> none  [the longest x1 20.9 us: per_device(): lax.psum((query_part, keyval_part, jnp.sum(resid * resid, axis=1)), 'wide')]
    pallas_call x0 -> x1, Pallas kernels: none -> 47.8 us  [per_device(): pl.pallas_call(functools.partial(kernel, plan), out_shape=jax.ShapeDtypeS...]
    all_gather x5 -> x0, blocking collectives: 46.2 us -> none  [the longest x3 42.6 us: combined_all(): gathered = jax.tree.map(lambda a: lax.all_gather(a, axis), part)]
    dot_general x8 -> x0, matrix products: 43.1 us -> none  [the longest x1 10.4 us: per_device(): jnp.dot(activated, down_weight, preferred_element_type=jnp.float32)]
    psum x1 -> x0, waiting for transfers between devices: 36.5 us -> none  [per_device(): lax.psum((gate_part, up_part, squares2), ('wide', 'sub'))]
    convert_element_type x7 -> x0, other arithmetic: 2.91 us -> none  [the longest x1 0.75 us: per_device(): resid = residual.astype(jnp.float32)]
    reshape x1 -> x2, local copies, waits for them, and re-layouts: 0.02 us -> 2.57 us  [the longest x1 1.3 us: per_device(): attn_gain.reshape(1, -1)]
  transfers between devices with their start and end apart: 1 -> 0, of which waited for: 1 -> 0; matrix products, arithmetic and copies ran while one was open for 0% -> 0% of each run, Pallas kernels for 0% -> 0%
where the time goes in v1:
time: 52.1 us; the launch traced here: 51.7 us
  Pallas kernels  47.8 us (92%)
  local copies, waits for them, and re-layouts  3.89 us (7%)
    pallas_call x1, Pallas kernels, per_device(): pl.pallas_call(functools.partial(kernel, plan), out_shape=jax.ShapeDtypeS...  47.8 us
    unnamed x1, local copies, waits for them, and re-layouts  1.31 us
    reshape x1, local copies, waits for them, and re-layouts, per_device(): attn_gain.reshape(1, -1)  1.3 us
    reshape x1, local copies, waits for them, and re-layouts, per_device(): ffn_gain.reshape(1, -1)  1.28 us

profile of v1, /device:TPU:0, one launch (start us, length us, event | category | flops | bytes accessed | tf_op | source)
XLA Modules:
  0.0 51.7 jit_solution(17077793127252584752)
XLA Ops:
  0.0 1.3 %reshape.7.ffn_ref = bf16[1,1536]{1,0:T(2,128)(2,1)} reshape(bf16[1536]{0:T(1024)(128)(2,1)} %param.22) | data formatting | bytes 6144 | tf_op jit(solution)/shard_map/reshape | solution.py:622
  1.3 1.3 %reshape.6.attn_ref = bf16[1,3072]{1,0:T(2,128)(2,1)} reshape(bf16[3072]{0:T(1024)(128)(2,1)} %param.14) | data formatting | bytes 12288 | tf_op jit(solution)/shard_map/reshape | solution.py:622
  2.6 47.8 %layer.1 = bf16[4,1536]{1,0:T(4,128)(2,1)} custom-call(bf16[4,3072]{1,0:T(4,128)(2,1)} %res_ref.1, bf16[1,3072]{1,0:T(2,128)(2,1)} %reshape.6.attn_ref, bf16[1,1536]{1,0:T(2,128)(2,1)} %reshape.7.ffn_ref, s32[4]{0:T(128)} %len_ref.1, s32[4]{0:T(128)} %pos_ref.1, bf16[3072,1536]{1,0:T(8,128)(2,1)} %query_hbm.1, bf16[3072,256]{1,0:T(8,128)(2,1)} %keyval_hbm.1, ...), custom_call_target="tpu_custom_call" | custom-call | tf_op jit(solution)/shard_map/layer/pallas_call | solution.py:611
  50.4 1.3 %copy.15 = bf16[4,1536]{1,0:T(4,128)(2,1)} copy(bf16[4,1536]{1,0:T(4,128)(2,1)} %layer.1) | data formatting | bytes 24576

commit v2 on v1

--- a/solution.py
+++ b/solution.py
@@ -14,8 +14,8 @@
 lane = 128
 bf16 = jnp.bfloat16
 f32 = jnp.float32
-weight_budget = 60 * 2**20
 vmem_limit = 63 * 2**20
+lag = 2
 
 
 def split_two(value):
@@ -29,7 +29,7 @@
 
 class Plan:
     def __init__(self, sizes, residual, query, keyval, output, cache, gate, down):
-        self.wide, self.short, self.sub = sizes
+        self.wide, self.short, self.sub, self.pair = sizes
         self.members = self.wide * self.sub
         self.answers, self.width = residual
         self.groups = 16 // self.answers
@@ -43,29 +43,18 @@
         self.rows = cache[2]
         self.units = self.sub * self.head_tiles
         self.out_rows, self.out_cols = output
-        self.gate_rows, self.ff = gate
+        self.gate_rows, whole_ff = gate
+        self.ff = whole_ff // self.pair
+        self.all_answers = self.answers * self.pair
+        self.folds = 16 // self.all_answers
+        self.planes = self.pair * self.short
         self.owners = largest_divisor(self.ff // lane, self.members)
         self.piece = self.ff // self.owners
         self.tiles = self.piece // lane
-        self.half = -(-(self.tiles + 1) // self.groups) * lane
+        self.half = -(-(self.tiles + 1) // self.folds) * lane
         self.query_chunks = largest_divisor(self.width // lane, 6)
         self.out_chunks = largest_divisor(self.out_rows // lane, 6)
-        fixed = 2 * (
-            query[0] * query[1] + keyval[0] * keyval[1] + output[0] * output[1]
-            + 2 * math.prod(cache)
-        )
-        slot = 2 * self.gate_rows * 2 * self.piece
-        self.slots = min(self.members, (weight_budget - fixed) // slot)
-        in_query = self.width // self.piece if self.query_cols >= self.out_cols else 0
-        in_out = self.out_rows // self.piece
-        places = [("query", k) for k in range(in_query)] + [("out", k) for k in range(in_out)]
-        places = places[: self.members]
-        left = self.members - len(places)
-        fits = self.piece <= self.gate_rows and self.out_cols <= 2 * self.piece
-        kind = "slot" if fits and left <= self.slots else "extra"
-        places += [(kind, k) for k in range(left)]
-        self.places = places
-        self.extra = max(left * self.piece, 16) if kind == "extra" else 16
+        assert self.all_answers * self.folds == 16 and self.ff * self.pair == whole_ff
         assert self.units <= self.members and self.sub % self.kv_heads == 0
         assert self.blocks * self.sub == 2 * self.kv_heads
 
@@ -75,28 +64,25 @@
     res_ref, attn_ref, ffn_ref, len_ref, pos_ref,
     query_hbm, keyval_hbm, output_hbm, keys_hbm, values_hbm, gate_hbm, up_hbm, down_hbm,
     out_ref,
-    query_buf, keyval_buf, output_buf, keys_buf, values_buf, ffn_buf, extra_buf,
+    query_buf, keyval_buf, output_buf, keys_buf, values_buf, ffn_buf, down_buf,
     normed_ref, pack_ref, spread_ref, kv_ref, new_key_ref, new_value_ref,
     send1, recv1, rot, pay, recv_pay, att, out_lhs, wide_acc,
-    part_send, part_recv, normed2_ref, hidden_ref, square_ref,
-    ffn_pack, ffn_send, ffn_recv, act, down_lhs, last_send, last_recv,
+    part_all, normed2_ref, hidden_ref, both_ref, square_ref,
+    ffn_pack, ffn_sum, ffn_send, ffn_recv, act, down_lhs, last_part, last_recv,
     query_sem, keyval_sem, cache_sem, output_sem, ffn_sem, down_sem,
     s1, r1, s2, r2, s3, r3, s4, r4, s5, r5, s6, r6, s7, r7, s8, r8,
 ):
     n, wides, shorts, subs = plan.members, plan.wide, plan.short, plan.sub
     answers, groups = plan.answers, plan.groups
     wide, short, sub = lax.axis_index("wide"), lax.axis_index("short"), lax.axis_index("sub")
+    part = lax.axis_index("groups")
+    planes = plan.planes
+    plane = part * shorts + short
     me = wide * subs + sub
-    all_own = plan.owners == n
+    owners = plan.owners
 
     def member(rank):
         return {"wide": rank // subs, "sub": rank % subs}
-
-    def owned(rank, body):
-        if all_own:
-            body()
-        else:
-            pl.when(rank < plan.owners)(body)
 
     def remote(src, dst, ssem, rsem, device):
         return pltpu.make_async_remote_copy(
@@ -110,9 +96,12 @@
             barrier, inc=1, device_id=member(lax.rem(me + o, n)),
             device_id_type=pl.DeviceIdType.MESH,
         )
-    for o in range(1, shorts):
+    def in_plane(rank):
+        return {"groups": rank // shorts, "short": rank % shorts}
+
+    for o in range(1, planes):
         pl.semaphore_signal(
-            barrier, inc=1, device_id={"short": lax.rem(short + o, shorts)},
+            barrier, inc=1, device_id=in_plane(lax.rem(plane + o, planes)),
             device_id_type=pl.DeviceIdType.MESH,
         )
 
@@ -131,53 +120,38 @@
     keys_copy = pltpu.make_async_copy(keys_hbm, keys_buf, cache_sem.at[0])
     values_copy = pltpu.make_async_copy(values_hbm, values_buf, cache_sem.at[1])
 
-    def ffn_rank(i):
-        return lax.rem(me + 1 + i, n)
-
     def ffn_copies(i):
-        slot = lax.rem(i, plan.slots)
-        at = pl.ds(pl.multiple_of(ffn_rank(i) * plan.piece, lane), plan.piece)
+        at = pl.ds(pl.multiple_of(part * plan.ff + i * plan.piece, lane), plan.piece)
         return [
             pltpu.make_async_copy(
                 hbm.at[:, at],
-                ffn_buf.at[slot, :, pl.ds(k * plan.piece, plan.piece)],
-                ffn_sem.at[slot, k],
+                ffn_buf.at[i, :, pl.ds(k * plan.piece, plan.piece)],
+                ffn_sem.at[i, k],
             )
             for k, hbm in enumerate((gate_hbm, up_hbm))
         ]
 
     def ffn_start(i):
-        def body():
-            for copy in ffn_copies(i):
-                copy.start()
-
-        owned(ffn_rank(i), body)
-
-    def down_rank(j):
-        return lax.rem(me - j + n, n)
-
-    def down_place(j):
-        kind, k = plan.places[j]
-        if kind == "slot":
-            at = (n - plan.slots + k) % plan.slots
-            return ffn_buf.at[at, pl.ds(0, plan.piece), pl.ds(0, plan.out_cols)]
-        buf = {"query": query_buf, "out": output_buf, "extra": extra_buf}[kind]
-        return buf.at[pl.ds(k * plan.piece, plan.piece), pl.ds(0, plan.out_cols)]
+        for copy in ffn_copies(i):
+            copy.start()
 
     def down_copy(j):
-        at = pl.ds(pl.multiple_of(down_rank(j) * plan.piece, lane), plan.piece)
-        return pltpu.make_async_copy(down_hbm.at[at], down_place(j), down_sem.at[j])
-
-    def down_start(j):
-        owned(down_rank(j), lambda: down_copy(j).start())
+        at = pl.ds(pl.multiple_of(part * plan.ff + j * plan.piece, lane), plan.piece)
+        here = pl.ds(pl.multiple_of(j * plan.piece, lane), plan.piece)
+        return pltpu.make_async_copy(down_hbm.at[at], down_buf.at[here], down_sem.at[j])
 
     keyval_copy.start()
     for c in range(plan.query_chunks):
         query_copy(c).start()
     keys_copy.start()
     values_copy.start()
-    queue = [functools.partial(lambda c: output_copy(c).start(), c) for c in range(plan.out_chunks)]
-    queue += [functools.partial(ffn_start, i) for i in range(plan.slots)]
+    begun = [0]
+
+    def ffn_begin(sevenths):
+        upto = -(-owners * sevenths // 7)
+        for i in range(begun[0], upto):
+            ffn_start(i)
+        begun[0] = upto
 
     resid = res_ref[...].astype(f32)
     normed_ref[...] = (resid * attn_ref[...].astype(f32)).astype(bf16)
@@ -200,18 +174,10 @@
     keyval_copy.wait()
     kv_part = jnp.dot(normed_ref[...], keyval_buf[...], preferred_element_type=f32)
     q_part = jnp.zeros((answers, plan.query_cols), f32)
-    share = -(-len(queue) // plan.query_chunks)
     for c in range(plan.query_chunks):
         query_copy(c).wait()
-        for _ in range(share):
-            if queue:
-                queue.pop(0)()
         at = pl.ds(c * q_rows, q_rows)
         q_part += jnp.dot(normed_ref[:, at], query_buf[at, :], preferred_element_type=f32)
-    for j, (kind, _) in enumerate(plan.places):
-        if kind in ("query", "extra"):
-            down_start(j)
-
     def place(k):
         g, first = k % groups, k // groups * lane
         return slice(g * answers, (g + 1) * answers), slice(first, first + lane)
@@ -226,7 +192,7 @@
         pack_ref[place(k)] = tile
     send1[...] = pack_ref[...].astype(bf16)
 
-    pl.semaphore_wait(barrier, n - 1 + shorts - 1)
+    pl.semaphore_wait(barrier, n - 1 + planes - 1)
 
     def copy1(o):
         return remote(
@@ -236,6 +202,8 @@
 
     for o in range(1, wides):
         copy1(o).start()
+    for c in range(plan.out_chunks):
+        output_copy(c).start()
     for o in range(1, wides):
         copy1(o).wait_recv()
         pack_ref[...] += recv1[o - 1].astype(f32)
@@ -265,6 +233,7 @@
 
     for o in range(1, subs):
         copy2(o, sub).start()
+    ffn_begin(1)
     for o in range(1, subs):
         copy2(o, lax.rem(sub - o + subs, subs)).wait_recv()
 
@@ -332,6 +301,8 @@
             def _():
                 copy3(u, me).start()
 
+    ffn_begin(3)
+
     def copy4(o, source):
         return remote(
             att.at[source], att.at[source], s4.at[o - 1], r4.at[source],
@@ -359,6 +330,7 @@
         for o in range(1, n):
             copy4(o, me).start()
 
+    ffn_begin(5)
     for u in range(plan.units):
 
         @pl.when(me != u)
@@ -380,137 +352,151 @@
         output_copy(c).wait()
         at = pl.ds(c * o_rows, o_rows)
         product += jnp.dot(out_lhs[:, at], output_buf[at, :], preferred_element_type=f32)
-    for j, (kind, _) in enumerate(plan.places):
-        if kind == "out":
-            down_start(j)
-
-    def folded(value):
+    def folded(value, rows):
         wide_acc[...] = value
         return functools.reduce(
-            jnp.add, [wide_acc[g * answers : (g + 1) * answers, :] for g in range(groups)]
-        )
-
-    def across_short(value, send, recv, ssem, rsem):
-        send[...] = value
-        copies = [
-            remote(
-                send, recv.at[o - 1], ssem.at[o - 1], rsem.at[o - 1],
-                {"short": lax.rem(short + o, shorts)},
-            )
-            for o in range(1, shorts)
-        ]
-        for copy in copies:
-            copy.start()
-        for o, copy in enumerate(copies):
-            copy.wait_recv()
-            value += recv[o]
-        return value
+            jnp.add, [wide_acc[r : r + rows, :] for r in range(0, 16, rows)]
+        )
 
     resid_part = res_ref[:, : plan.out_cols].astype(f32)
     for k in range(1, subs):
         here = res_ref[:, k * plan.out_cols : (k + 1) * plan.out_cols].astype(f32)
         resid_part = jnp.where(sub == k, here, resid_part)
-    hidden = resid_part + across_short(folded(product), part_send, part_recv, s5, r5)
-    hidden_ref[...] = hidden
-    normed2_ref[...] = (hidden * ffn_ref[...].astype(f32)).astype(bf16)
+    part_all[plane] = folded(product, answers) + jnp.where(short == 0, resid_part, 0.0)
+
+    def copy5(o, source):
+        return remote(
+            part_all.at[source], part_all.at[source], s5.at[o - 1], r5.at[source],
+            in_plane(lax.rem(plane + o, planes)),
+        )
+
+    for o in range(1, planes):
+        copy5(o, plane).start()
+    ffn_begin(7)
+    for o in range(1, planes):
+        copy5(o, lax.rem(plane + o, planes)).wait_recv()
+
+    for p in range(plan.pair):
+        hidden = functools.reduce(
+            jnp.add, [part_all[p * shorts + x] for x in range(shorts)]
+        )
+        rows = slice(p * answers, (p + 1) * answers)
+        hidden_ref[p] = hidden
+        both_ref[rows, :] = hidden
+    hidden = both_ref[...]
+    gain = jnp.broadcast_to(ffn_ref[...].astype(f32), hidden.shape)
+    normed2_ref[...] = (hidden * gain).astype(bf16)
     high, low = split_two(
-        jnp.broadcast_to(jnp.sum(hidden * hidden, axis=1, keepdims=True), (answers, lane))
+        jnp.broadcast_to(
+            jnp.sum(hidden * hidden, axis=1, keepdims=True), (plan.all_answers, lane)
+        )
     )
     square_ref[0] = high
     square_ref[1] = low
 
+    many, folds = plan.all_answers, plan.folds
+
     def ffn_place(t, k):
-        rows, columns = place(t)
-        first = columns.start + k * plan.half
-        return rows, slice(first, first + lane)
+        first = t // folds * lane + k * plan.half
+        return slice(t % folds * many, (t % folds + 1) * many), slice(first, first + lane)
 
     def ffn_piece(i):
-        slot = lax.rem(i, plan.slots)
         for copy in ffn_copies(i):
             copy.wait()
+        both = jnp.dot(
+            normed2_ref[...], ffn_buf[i], preferred_element_type=f32
+        )
         for k in range(2):
-            part = jnp.dot(
-                normed2_ref[...],
-                ffn_buf[slot, :, pl.ds(k * plan.piece, plan.piece)],
-                preferred_element_type=f32,
-            )
-            for t, tile in enumerate(tiles_of(part) + [square_ref[k]]):
+            mine = both[:, k * plan.piece : (k + 1) * plan.piece]
+            for t, tile in enumerate(tiles_of(mine) + [square_ref[k]]):
                 ffn_pack[ffn_place(t, k)] = tile
-
-    def copy6(i):
+        ffn_send[i] = ffn_pack[...].astype(bf16)
+
+    def copy6(i, source):
         return remote(
-            ffn_send.at[i], ffn_recv.at[i], s6.at[i], r6.at[i], member(ffn_rank(i))
-        )
-
-    def ffn_freed(i):
-        @pl.when(i + plan.slots < n)
-        def _():
-            ffn_start(i + plan.slots)
-
-        for j, (kind, k) in enumerate(plan.places):
-            if kind == "slot":
-
-                @pl.when(i == n - plan.slots + k)
-                def _():
-                    down_start(j)
-
-    def ffn_step(i, carry):
-        def body():
-            ffn_piece(i)
-            ffn_send[i] = ffn_pack[...].astype(bf16)
-            copy6(i).start()
-
-        owned(ffn_rank(i), body)
-        ffn_freed(i)
-        return carry
-
-    lax.fori_loop(0, n - 1, ffn_step, 0)
-
-    def copy7(o):
+            ffn_send.at[i], ffn_recv.at[source], s6.at[i], r6.at[source], member(i)
+        )
+
+    def copy7(o, source):
         return remote(
-            act.at[n - 1], act.at[o - 1], s7.at[o - 1], r7.at[o - 1],
+            act.at[source], act.at[source], s7.at[o - 1], r7.at[source],
             member(lax.rem(me + o, n)),
         )
 
     def activate():
-        ffn_piece(n - 1)
-        for i in range(n - 1):
-            copy6(i).wait_recv()
-            ffn_pack[...] += ffn_recv[i].astype(f32)
-        total2 = ffn_pack[ffn_place(plan.tiles, 0)] + ffn_pack[ffn_place(plan.tiles, 1)]
-        factor2 = spread(lax.rsqrt(total2 / plan.model + epsilon))
+        total2 = ffn_send[me].astype(f32)
+        for o in range(1, n):
+            source = lax.rem(me + o, n)
+            copy6(0, source).wait_recv()
+            total2 += ffn_recv[source].astype(f32)
+        ffn_sum[...] = total2
+        square = ffn_sum[ffn_place(plan.tiles, 0)] + ffn_sum[ffn_place(plan.tiles, 1)]
+        for g in range(folds):
+            spread_ref[g * many : (g + 1) * many, :] = lax.rsqrt(square / plan.model + epsilon)
+        factor2 = spread_ref[...]
         for t in range(plan.half // lane):
-            gate = ffn_pack[:, t * lane : (t + 1) * lane] * factor2
-            upward = ffn_pack[:, plan.half + t * lane : plan.half + (t + 1) * lane] * factor2
-            act[n - 1, :, t * lane : (t + 1) * lane] = (
+            gate = total2[:, t * lane : (t + 1) * lane] * factor2
+            upward = total2[:, plan.half + t * lane : plan.half + (t + 1) * lane] * factor2
+            act[me, :, t * lane : (t + 1) * lane] = (
                 gate / (1.0 + jnp.exp(-gate)) * upward
             ).astype(bf16)
         for o in range(1, n):
-            copy7(o).start()
-
-    owned(me, activate)
-    ffn_freed(n - 1)
+            copy7(o, me).start()
+
+    def ffn_step(i, carry):
+        ffn_piece(i)
+
+        @pl.when(me != i)
+        def _():
+            copy6(i, me).start()
+
+        down_copy(i).start()
+        pl.when(me == i - lag)(activate)
+        return carry
+
+    lax.fori_loop(0, owners, ffn_step, 0)
 
     wide_acc[...] = jnp.zeros_like(wide_acc)
-    for j in range(n):
-
-        def down_piece():
-            if j:
-                copy7(j).wait_recv()
-            down_copy(j).wait()
-            block = act[(j - 1) % n].astype(f32)
-            for k in range(plan.tiles):
-                first = (k // groups) * lane
-                down_lhs[:, k * lane : (k + 1) * lane] = jnp.where(
-                    group16 == k % groups, block[:, first : first + lane], 0.0
-                ).astype(bf16)
-            wide_acc[...] += jnp.dot(
-                down_lhs[...], down_place(j)[...], preferred_element_type=f32
-            )
-
-        owned(down_rank(j), down_piece)
-    projected = across_short(folded(wide_acc[...]), last_send, last_recv, s8, r8)
-    out_ref[...] = (hidden_ref[...] + projected).astype(bf16)
+    for j in range(owners):
+
+        @pl.when(me != j)
+        def _():
+            copy7(1, j).wait_recv()
+
+        down_copy(j).wait()
+        block = act[j].astype(f32)
+        for k in range(plan.tiles):
+            first = (k // folds) * lane
+            down_lhs[:, k * lane : (k + 1) * lane] = jnp.where(
+                row16 // many == k % folds, block[:, first : first + lane], 0.0
+            ).astype(bf16)
+        wide_acc[...] += jnp.dot(
+            down_lhs[...], down_buf[j * plan.piece : (j + 1) * plan.piece, :],
+            preferred_element_type=f32,
+        )
+        if j == 0:
+            pl.when(me == owners - 2)(activate)
+        if j == 2:
+            pl.when(me == owners - 1)(activate)
+    both_ref[...] = folded(wide_acc[...], many)
+    for p in range(plan.pair):
+        last_part[p] = both_ref[p * answers : (p + 1) * answers, :]
+
+    def copy8(o, source):
+        target = lax.rem(plane + o, planes)
+        return remote(
+            last_part.at[target // shorts], last_recv.at[source], s8.at[o - 1], r8.at[source],
+            in_plane(target),
+        )
+
+    for o in range(1, planes):
+        copy8(o, plane).start()
+    result = hidden_ref[part] + last_part[part]
+    for o in range(1, planes):
+        source = lax.rem(plane + o, planes)
+        copy8(o, source).wait_recv()
+        result += last_recv[source]
+    out_ref[...] = result.astype(bf16)
 
     for o in range(1, wides):
         copy1(o).wait_send()
@@ -527,22 +513,19 @@
         for o in range(1, n):
             copy4(o, me).wait_send()
 
-    for o in range(1, shorts):
-        for send, recv, ssem, rsem in (
-            (part_send, part_recv, s5, r5), (last_send, last_recv, s8, r8)
-        ):
-            remote(
-                send, recv.at[o - 1], ssem.at[o - 1], rsem.at[o - 1],
-                {"short": lax.rem(short + o, shorts)},
-            ).wait_send()
-    for i in range(n - 1):
-        owned(ffn_rank(i), lambda: copy6(i).wait_send())
-
-    def sent7():
+    for o in range(1, planes):
+        copy5(o, plane).wait_send()
+        copy8(o, plane).wait_send()
+    for i in range(owners):
+
+        @pl.when(me != i)
+        def _():
+            copy6(i, me).wait_send()
+
+    @pl.when(me < owners)
+    def _():
         for o in range(1, n):
-            copy7(o).wait_send()
-
-    owned(me, sent7)
+            copy7(o, me).wait_send()
 
 
 def per_device(
@@ -558,15 +541,14 @@
     smem = pl.BlockSpec(memory_space=pltpu.SMEM)
     hbm = pl.BlockSpec(memory_space=pltpu.HBM)
     dma = pltpu.SemaphoreType.DMA
-    short_peers = max(plan.short - 1, 1)
     scratch = [
         pltpu.VMEM(query_weight.shape, bf16),
         pltpu.VMEM(key_value_weight.shape, bf16),
         pltpu.VMEM(output_weight.shape, bf16),
         pltpu.VMEM(cache_keys.shape, bf16),
         pltpu.VMEM(cache_keys.shape, bf16),
-        pltpu.VMEM((plan.slots, plan.gate_rows, 2 * plan.piece), bf16),
-        pltpu.VMEM((plan.extra, plan.out_cols), bf16),
+        pltpu.VMEM((plan.owners, plan.gate_rows, 2 * plan.piece), bf16),
+        pltpu.VMEM((plan.ff, plan.out_cols), bf16),
         pltpu.VMEM((answers, plan.width), bf16),
         pltpu.VMEM((16, plan.pack_cols), f32),
         pltpu.VMEM((16, lane), f32),
@@ -581,32 +563,33 @@
         pltpu.VMEM((plan.units, 16, lane), bf16),
         pltpu.VMEM((16, plan.out_rows), bf16),
         pltpu.VMEM((16, plan.out_cols), f32),
-        pltpu.VMEM((answers, plan.out_cols), f32),
-        pltpu.VMEM((short_peers, answers, plan.out_cols), f32),
-        pltpu.VMEM((answers, plan.out_cols), bf16),
-        pltpu.VMEM((answers, plan.out_cols), f32),
-        pltpu.VMEM((2, answers, lane), f32),
+        pltpu.VMEM((plan.planes, answers, plan.out_cols), f32),
+        pltpu.VMEM((plan.all_answers, plan.out_cols), bf16),
+        pltpu.VMEM((plan.pair, answers, plan.out_cols), f32),
+        pltpu.VMEM((plan.all_answers, plan.out_cols), f32),
+        pltpu.VMEM((2, plan.all_answers, lane), f32),
         pltpu.VMEM((16, 2 * plan.half), f32),
-        pltpu.VMEM((n - 1, 16, 2 * plan.half), bf16),
-        pltpu.VMEM((n - 1, 16, 2 * plan.half), bf16),
-        pltpu.VMEM((n, 16, plan.half), bf16),
+        pltpu.VMEM((16, 2 * plan.half), f32),
+        pltpu.VMEM((plan.owners, 16, 2 * plan.half), bf16),
+        pltpu.VMEM((n, 16, 2 * plan.half), bf16),
+        pltpu.VMEM((plan.owners, 16, plan.half), bf16),
         pltpu.VMEM((16, plan.piece), bf16),
-        pltpu.VMEM((answers, plan.out_cols), f32),
-        pltpu.VMEM((short_peers, answers, plan.out_cols), f32),
+        pltpu.VMEM((plan.pair, answers, plan.out_cols), f32),
+        pltpu.VMEM((plan.planes, answers, plan.out_cols), f32),
         dma((plan.query_chunks,)),
         dma((1,)),
         dma((2,)),
         dma((plan.out_chunks,)),
-        dma((plan.slots, 2)),
-        dma((n,)),
+        dma((plan.owners, 2)),
+        dma((plan.owners,)),
         dma((plan.wide - 1,)), dma((plan.wide - 1,)),
         dma((plan.sub - 1,)), dma((plan.sub - 1,)),
         dma((plan.units,)), dma((n,)),
         dma((n - 1,)), dma((plan.units,)),
-        dma((short_peers,)), dma((short_peers,)),
-        dma((n - 1,)), dma((n - 1,)),
-        dma((n - 1,)), dma((n - 1,)),
-        dma((short_peers,)), dma((short_peers,)),
+        dma((plan.planes,)), dma((plan.planes,)),
+        dma((plan.owners,)), dma((n,)),
+        dma((n - 1,)), dma((plan.owners,)),
+        dma((plan.planes,)), dma((plan.planes,)),
     ]
     return pl.pallas_call(
         functools.partial(kernel, plan),
@@ -619,14 +602,14 @@
         ),
         name="layer",
     )(
-        residual, attn_gain.reshape(1, -1), ffn_gain.reshape(1, -1), lengths, positions,
+        residual, attn_gain, ffn_gain, lengths, positions,
         query_weight, key_value_weight, output_weight, cache_keys, cached_value_rows,
         gate_weight, up_weight, down_weight,
     )
 
 
 def solution(mesh):
-    sizes = (mesh.shape["wide"], mesh.shape["short"], mesh.shape["sub"])
+    sizes = tuple(mesh.shape[name] for name in ("wide", "short", "sub", "groups"))
     placed = (
         P("groups", "wide"),
         P("wide"),

time: 52.1 us -> 53.4 us (1.025)
  Pallas kernels: 47.8 us -> 51.8 us
  local copies, waits for them, and re-layouts: 3.89 us -> 1.31 us
    pallas_call x1, Pallas kernels: 47.8 us -> 51.8 us  [per_device(): pl.pallas_call(functools.partial(kernel, plan), out_shape=jax.ShapeDtypeS...]
    reshape x2 -> x0, local copies, waits for them, and re-layouts: 2.57 us -> none  [the longest x1 1.3 us: per_device(): attn_gain.reshape(1, -1)]
where the time goes in v2:
time: 53.4 us; the launch traced here: 53.1 us
  Pallas kernels  51.8 us (97%)
  local copies, waits for them, and re-layouts  1.31 us (2%)
    pallas_call x1, Pallas kernels, per_device(): pl.pallas_call(functools.partial(kernel, plan), out_shape=jax.ShapeDtypeS...  51.8 us
    unnamed x1, local copies, waits for them, and re-layouts  1.31 us

profile of v2, /device:TPU:0, one launch (start us, length us, event | category | flops | bytes accessed | tf_op | source)
XLA Modules:
  0.0 53.1 jit_solution(5114636497226245786)
XLA Ops:
  0.0 51.8 %layer.1 = bf16[4,1536]{1,0:T(4,128)(2,1)} custom-call(bf16[4,3072]{1,0:T(4,128)(2,1)} %res_ref.1, bf16[3072]{0:T(1024)(128)(2,1)} %attn_ref.1, bf16[1536]{0:T(1024)(128)(2,1)} %ffn_ref.1, s32[4]{0:T(128)} %len_ref.1, s32[4]{0:T(128)} %pos_ref.1, bf16[3072,1536]{1,0:T(8,128)(2,1)} %query_hbm.1, bf16[3072,256]{1,0:T(8,128)(2,1)} %keyval_hbm.1, ...), custom_call_target="tpu_custom_call" | custom-call | tf_op jit(solution)/shard_map/layer/pallas_call | solution.py:594
  51.8 1.3 %copy.15 = bf16[4,1536]{1,0:T(4,128)(2,1)} copy(bf16[4,1536]{1,0:T(4,128)(2,1)} %layer.1) | data formatting | bytes 24576

commit v3 on v2

--- a/solution.py
+++ b/solution.py
@@ -15,7 +15,6 @@
 bf16 = jnp.bfloat16
 f32 = jnp.float32
 vmem_limit = 63 * 2**20
-lag = 2
 
 
 def split_two(value):
@@ -54,7 +53,7 @@
         self.half = -(-(self.tiles + 1) // self.folds) * lane
         self.query_chunks = largest_divisor(self.width // lane, 6)
         self.out_chunks = largest_divisor(self.out_rows // lane, 6)
-        assert self.all_answers * self.folds == 16 and self.ff * self.pair == whole_ff
+        assert self.members < 3 * self.owners and self.all_answers * self.folds == 16 and self.ff * self.pair == whole_ff
         assert self.units <= self.members and self.sub % self.kv_heads == 0
         assert self.blocks * self.sub == 2 * self.kv_heads
 
@@ -120,8 +119,15 @@
     keys_copy = pltpu.make_async_copy(keys_hbm, keys_buf, cache_sem.at[0])
     values_copy = pltpu.make_async_copy(values_hbm, values_buf, cache_sem.at[1])
 
+    def ffn_owner(i):
+        return lax.rem(me + 1 + i, owners)
+
+    def down_owner(j):
+        return lax.rem(me - j + 2 * owners, owners)
+
     def ffn_copies(i):
-        at = pl.ds(pl.multiple_of(part * plan.ff + i * plan.piece, lane), plan.piece)
+        first = part * plan.ff + ffn_owner(i) * plan.piece
+        at = pl.ds(pl.multiple_of(first, lane), plan.piece)
         return [
             pltpu.make_async_copy(
                 hbm.at[:, at],
@@ -136,7 +142,8 @@
             copy.start()
 
     def down_copy(j):
-        at = pl.ds(pl.multiple_of(part * plan.ff + j * plan.piece, lane), plan.piece)
+        first = part * plan.ff + down_owner(j) * plan.piece
+        at = pl.ds(pl.multiple_of(first, lane), plan.piece)
         here = pl.ds(pl.multiple_of(j * plan.piece, lane), plan.piece)
         return pltpu.make_async_copy(down_hbm.at[at], down_buf.at[here], down_sem.at[j])
 
@@ -410,7 +417,7 @@
             mine = both[:, k * plan.piece : (k + 1) * plan.piece]
             for t, tile in enumerate(tiles_of(mine) + [square_ref[k]]):
                 ffn_pack[ffn_place(t, k)] = tile
-        ffn_send[i] = ffn_pack[...].astype(bf16)
+        ffn_send[ffn_owner(i)] = ffn_pack[...].astype(bf16)
 
     def copy6(i, source):
         return remote(
@@ -446,25 +453,28 @@
     def ffn_step(i, carry):
         ffn_piece(i)
 
-        @pl.when(me != i)
+        owner = ffn_owner(i)
+
+        @pl.when(me != owner)
         def _():
-            copy6(i, me).start()
+            copy6(owner, me).start()
 
         down_copy(i).start()
-        pl.when(me == i - lag)(activate)
         return carry
 
     lax.fori_loop(0, owners, ffn_step, 0)
+    pl.when(me < owners)(activate)
 
     wide_acc[...] = jnp.zeros_like(wide_acc)
     for j in range(owners):
-
-        @pl.when(me != j)
+        owner = down_owner(j)
+
+        @pl.when(me != owner)
         def _():
-            copy7(1, j).wait_recv()
+            copy7(1, owner).wait_recv()
 
         down_copy(j).wait()
-        block = act[j].astype(f32)
+        block = act[owner].astype(f32)
         for k in range(plan.tiles):
             first = (k // folds) * lane
             down_lhs[:, k * lane : (k + 1) * lane] = jnp.where(
@@ -474,10 +484,6 @@
             down_lhs[...], down_buf[j * plan.piece : (j + 1) * plan.piece, :],
             preferred_element_type=f32,
         )
-        if j == 0:
-            pl.when(me == owners - 2)(activate)
-        if j == 2:
-            pl.when(me == owners - 1)(activate)
     both_ref[...] = folded(wide_acc[...], many)
     for p in range(plan.pair):
         last_part[p] = both_ref[p * answers : (p + 1) * answers, :]

time: 53.4 us -> 48.5 us (0.908)
  Pallas kernels: 51.8 us -> 47 us
    pallas_call x1, Pallas kernels: 51.8 us -> 47 us  [per_device(): pl.pallas_call(functools.partial(kernel, plan), out_shape=jax.ShapeDtypeS...]
where the time goes in v3:
time: 48.5 us; the launch traced here: 48.3 us
  Pallas kernels  47 us (97%)
  local copies, waits for them, and re-layouts  1.31 us (3%)
    pallas_call x1, Pallas kernels, per_device(): pl.pallas_call(functools.partial(kernel, plan), out_shape=jax.ShapeDtypeS...  47 us
    unnamed x1, local copies, waits for them, and re-layouts  1.31 us

profile of v3, /device:TPU:0, one launch (start us, length us, event | category | flops | bytes accessed | tf_op | source)
XLA Modules:
  0.0 48.3 jit_solution(369899918577027520)
XLA Ops:
  0.0 47.0 %layer.1 = bf16[4,1536]{1,0:T(4,128)(2,1)} custom-call(bf16[4,3072]{1,0:T(4,128)(2,1)} %res_ref.1, bf16[3072]{0:T(1024)(128)(2,1)} %attn_ref.1, bf16[1536]{0:T(1024)(128)(2,1)} %ffn_ref.1, s32[4]{0:T(128)} %len_ref.1, s32[4]{0:T(128)} %pos_ref.1, bf16[3072,1536]{1,0:T(8,128)(2,1)} %query_hbm.1, bf16[3072,256]{1,0:T(8,128)(2,1)} %keyval_hbm.1, ...), custom_call_target="tpu_custom_call" | custom-call | tf_op jit(solution)/shard_map/layer/pallas_call | solution.py:600
  47.0 1.3 %copy.15 = bf16[4,1536]{1,0:T(4,128)(2,1)} copy(bf16[4,1536]{1,0:T(4,128)(2,1)} %layer.1) | data formatting | bytes 24576
